TPU v7x, 32 devices: a whole 2x2x4 slice. The times are simulated.
32 devices in a mesh: grp: 2 (over x), seq: 8 (over z, y), tp: 2 (over core).
Axes of the slice: x: 2, y: 2, z: 4, core: 2. Of those that a mesh axis runs over, the one named last changes fastest.
Arguments:
- queries: bfloat16 [2048, 5120], P(('grp', 'seq'), 'tp'), parts along dimension 0, may hold values from -80 to 80
- key_heads: bfloat16 [2048, 1024], P(('grp', 'seq'), 'tp'), parts along dimension 0, may hold values from -6 to 6
- values: bfloat16 [2048, 1024], P(('grp', 'seq'), 'tp'), parts along dimension 0, may hold values from -6 to 6
- residual: bfloat16 [2048, 5120], P(('grp', 'seq'), 'tp'), parts along dimension 0, may hold values from -4 to 4
- doc_start: int32 [2048], P(('grp', 'seq')), parts along dimension 0, may hold values from 0 to 1023, as said below
- norm_gain: bfloat16 [5120], P('tp'), may hold values from 0.5 to 1.5
- router: bfloat16 [5120, 4], P('tp'), may hold values from -0.078125 to 0.078125
- expert_id: int32 [2048], P(('grp', 'seq')), parts along dimension 0, may hold values from 0 to 3, as said below
- slot_index: int32 [2048], P(('grp', 'seq')), parts along dimension 0, may hold values from 0 to 47, as said below
- gate_weight: bfloat16 [5120, 16384], P('tp', 'seq'), may hold values from -0.078125 to 0.078125
- up_weight: bfloat16 [5120, 16384], P('tp', 'seq'), may hold values from -0.078125 to 0.078125
- down_weight: bfloat16 [16384, 5120], P('seq', 'tp'), may hold values from -0.09375 to 0.09375
Outputs:
- layer_out: bfloat16 [2048, 5120], P(('grp', 'seq'), 'tp'), parts along dimension 0
There are 2 independent parts, one for each index of `grp`. A program takes and returns all parts, laid end to end along the dimension named above; an argument that names none is the same for every part. Nothing has to cross between parts.
Inputs may be any that keep to these rules, and one draw needn't show every extreme that they name: Document starts never fall along the sequence and doc_start[t] <= t. `expert_id`: among the tokens of one index of seq no expert is named more than 48 times, and one expert is named exactly 48 times in every such block. `slot_index`: tokens of one index of seq that name the same expert have distinct slots.
All inputs are finite; a program needn't handle non-finite values.
Results may differ from a plain program's by a relative error of at most 0.008.
Values may be sent and summed in bfloat16 or wider, within the bound.
A program may use at most 128 MiB of HBM per device.

v0:
```python
import math

import jax
import jax.numpy as jnp
from jax import lax
from jax.sharding import PartitionSpec as P

D = 5120
QH = 40
KVH = 8
HD = 128
STRETCH_DEVS = 4


def shifted(array, axis, by):
    devices = lax.axis_size(axis)
    pairs = [(i, i + by) for i in range(devices) if 0 <= i + by < devices]
    return lax.ppermute(array, axis, pairs)


def on_device(
    queries,
    key_heads,
    values,
    residual,
    doc_start,
    norm_gain,
    router,
    expert_id,
    slot_index,
    gate_weight,
    up_weight,
    down_weight,
):
    tokens_dev = queries.shape[0]
    per_group = QH // KVH
    kv_local = key_heads.shape[1] // HD
    stretch_len = STRETCH_DEVS * tokens_dev
    score_scale = 1.0 / math.sqrt(HD)
    device = lax.axis_index("seq")
    own_block = (key_heads, values)
    blocks = []
    carried = own_block
    for distance in range(1, STRETCH_DEVS):
        carried = shifted((carried[0], carried[1]), "seq", 1)
        blocks.append(carried)
    ordered = blocks[::-1] + [own_block]
    key_all = jnp.concatenate([piece[0] for piece in ordered], 0).reshape(-1, kv_local, HD)
    value_all = jnp.concatenate([piece[1] for piece in ordered], 0).reshape(-1, kv_local, HD)
    query_view = queries.reshape(tokens_dev, kv_local, per_group, HD)
    scores = (
        jnp.einsum("tkgd,skd->kgts", query_view, key_all, preferred_element_type=jnp.float32)
        * score_scale
    )
    query_pos = device * tokens_dev + jnp.arange(tokens_dev, dtype=jnp.int32)
    key_pos = (device - (STRETCH_DEVS - 1)) * tokens_dev + jnp.arange(
        STRETCH_DEVS * tokens_dev, dtype=jnp.int32
    )
    allowed = (
        (key_pos[None, :] <= query_pos[:, None])
        & (key_pos[None, :] // stretch_len == query_pos[:, None] // stretch_len)
        & (key_pos[None, :] >= doc_start[:, None])
    )
    masked = jnp.where(allowed, scores, -jnp.inf)
    largest = jnp.max(masked, axis=-1, keepdims=True)
    exponent = jnp.exp(masked - largest)
    denominator = jnp.sum(exponent, axis=-1, keepdims=True)
    probabilities = exponent.astype(jnp.bfloat16)
    attended = jnp.einsum(
        "kgts,skd->tkgd", probabilities, value_all, preferred_element_type=jnp.float32
    )
    attended = (attended / jnp.transpose(denominator, (2, 0, 1, 3))).reshape(tokens_dev, -1)
    hidden_state = (residual.astype(jnp.float32) + attended).astype(jnp.bfloat16)
    gained = (hidden_state.astype(jnp.float32) * norm_gain.astype(jnp.float32)).astype(jnp.bfloat16)
    square_part = jnp.sum(jnp.square(hidden_state.astype(jnp.float32)), axis=1)
    logit_part = jnp.dot(gained, router, preferred_element_type=jnp.float32)
    square_sum, logit_sum = lax.psum((square_part, logit_part), "tp")
    inverse = lax.rsqrt(square_sum / D + 1e-05)
    experts_all = router.shape[1]
    chosen = expert_id[:, None] == jnp.arange(experts_all, dtype=jnp.int32)[None, :]
    picked = jnp.sum(jnp.where(chosen, inverse[:, None] * logit_sum, 0.0), axis=1)
    factor = inverse * jax.nn.sigmoid(picked)
    expert_in = (gained.astype(jnp.float32) * factor[:, None]).astype(jnp.bfloat16)
    capacity = 3 * tokens_dev // (2 * experts_all)
    slices_per_expert = lax.axis_size("seq") // experts_all
    features = expert_in.shape[1]
    place = expert_id * capacity + slot_index
    buffer = jnp.zeros((experts_all * capacity, features), jnp.bfloat16).at[place].set(expert_in)
    buffer = buffer.reshape(experts_all, capacity, features)
    outgoing = jnp.repeat(buffer, slices_per_expert, axis=0)
    arrived = lax.all_to_all(outgoing, "seq", split_axis=0, concat_axis=0, tiled=True)
    gate_part = jnp.einsum("scd,df->scf", arrived, gate_weight, preferred_element_type=jnp.float32)
    up_part = jnp.einsum("scd,df->scf", arrived, up_weight, preferred_element_type=jnp.float32)
    gate_full, up_full = lax.psum((gate_part, up_part), "tp")
    activated = (jax.nn.silu(gate_full) * up_full).astype(jnp.bfloat16)
    produced = jnp.einsum(
        "scf,fd->scd", activated, down_weight, preferred_element_type=jnp.float32
    ).astype(jnp.bfloat16)
    returned = lax.all_to_all(produced, "seq", split_axis=0, concat_axis=0, tiled=True)
    summed = jnp.sum(
        returned.reshape(experts_all, slices_per_expert, capacity, -1).astype(jnp.float32), axis=1
    )
    expert_out = summed.reshape(experts_all * capacity, -1)[place]
    return (hidden_state.astype(jnp.float32) + expert_out).astype(jnp.bfloat16)


def solution(mesh):
    return jax.shard_map(
        on_device,
        mesh=mesh,
        in_specs=(
            P(("grp", "seq"), "tp"),
            P(("grp", "seq"), "tp"),
            P(("grp", "seq"), "tp"),
            P(("grp", "seq"), "tp"),
            P(("grp", "seq")),
            P("tp"),
            P("tp", None),
            P(("grp", "seq")),
            P(("grp", "seq")),
            P("tp", "seq"),
            P("tp", "seq"),
            P("seq", "tp"),
        ),
        out_specs=P(("grp", "seq"), "tp"),
        check_vma=False,
    )
```

profile of v0, /device:TPU:0, one launch (start us, length us, event | category | flops | bytes accessed | tf_op | source)
XLA Modules:
  0.0 219.7 jit_solution(14935705414109869748)
XLA Ops:
  6.5 1.0 copy.18
  7.6 4.9 %collective-permute-start.3 = (bf16[128,512]{0,1:T(8,128)(2,1)S(1)}, bf16[128,512]{0,1:T(8,128)(2,1)S(1)}, u32[]{:S(2)}, u32[]{:S(2)}) collective-permute-start(bf16[128,512]{0,1:T(8,128)(2,1)S(1)} %copy.18), channel_id=1, source_target_pairs={{0,2},{2,4},{4,6},{6,8},{8,10},{10,12},{12,14},{1,3},{3,5},{5,7},{... | collective-permute-start | bytes 393224 | tf_op jit(solution)/shard_map/ppermute | solution.py:18
  12.5 3.4 %collective-permute-start = (bf16[128,512]{1,0:T(8,128)(2,1)}, bf16[128,512]{1,0:T(8,128)(2,1)S(1)}, u32[]{:S(2)}, u32[]{:S(2)}) collective-permute-start(bf16[128,512]{1,0:T(8,128)(2,1)} %param.14), channel_id=1, source_target_pairs={{0,2},{2,4},{4,6},{6,8},{8,10},{10,12},{12,14},{1,3},{3,5},{5,7},{... | collective-permute-start | bytes 393224 | tf_op jit(solution)/shard_map/ppermute | solution.py:18
  16.0 3.6 %collective-permute-start.4 = (bf16[128,512]{0,1:T(8,128)(2,1)S(1)}, bf16[128,512]{0,1:T(8,128)(2,1)S(1)}, u32[]{:S(2)}, u32[]{:S(2)}) collective-permute-start(bf16[128,512]{0,1:T(8,128)(2,1)S(1)} %collective-permute-done.3), channel_id=1, source_target_pairs={{0,2},{2,4},{4,6},{6,8},{8,10},{10,12},{12,14},{1,3},{3,5},{5,7},{... | collective-permute-start | bytes 393224 | tf_op jit(solution)/shard_map/ppermute | solution.py:18
  19.6 4.3 %collective-permute-start.1 = (bf16[128,512]{1,0:T(8,128)(2,1)S(1)}, bf16[128,512]{1,0:T(8,128)(2,1)S(1)}, u32[]{:S(2)}, u32[]{:S(2)}) collective-permute-start(bf16[128,512]{1,0:T(8,128)(2,1)S(1)} %collective-permute-done), channel_id=1, source_target_pairs={{0,2},{2,4},{4,6},{6,8},{8,10},{10,12},{12,14},{1,3},{3,5},{5,7},{... | collective-permute-start | bytes 393224 | tf_op jit(solution)/shard_map/ppermute | solution.py:18
  24.8 3.4 %collective-permute-start.5 = (bf16[128,512]{0,1:T(8,128)(2,1)S(1)}, bf16[128,512]{0,1:T(8,128)(2,1)S(1)}, u32[]{:S(2)}, u32[]{:S(2)}) collective-permute-start(bf16[128,512]{0,1:T(8,128)(2,1)S(1)} %collective-permute-done.4), channel_id=1, source_target_pairs={{0,2},{2,4},{4,6},{6,8},{8,10},{10,12},{12,14},{1,3},{3,5},{5,7},{... | collective-permute-start | bytes 393224 | tf_op jit(solution)/shard_map/ppermute | solution.py:18
  28.2 4.1 %collective-permute-start.2 = (bf16[128,512]{1,0:T(8,128)(2,1)S(1)}, bf16[128,512]{1,0:T(8,128)(2,1)S(1)}, u32[]{:S(2)}, u32[]{:S(2)}) collective-permute-start(bf16[128,512]{1,0:T(8,128)(2,1)S(1)} %collective-permute-done.1), channel_id=1, source_target_pairs={{0,2},{2,4},{4,6},{6,8},{8,10},{10,12},{12,14},{1,3},{3,5},{5,7},{... | collective-permute-start | bytes 393224 | tf_op jit(solution)/shard_map/ppermute | solution.py:18
  33.0 1.4 copy.20
  35.1 0.9 pad_maximum_fusion
  36.3 0.9 fusion.11
  37.3 1.1 fusion.6
  38.3 1.5 fusion.25
  40.8 2.5 %all-reduce = (f32[128,4]{0,1:T(4,128)S(1)}, f32[128]{0:T(128)S(1)}) all-reduce(f32[128,4]{0,1:T(4,128)S(1)} %fusion.30, f32[128]{0:T(128)S(1)} %get-tuple-element.9), channel_id=1, replica_groups=mesh['grp'=2,'seq'=8,'tp'=2] {'tp'}, use_global_device_ids=true, to_apply=%region_4.5 | all-reduce | flops 640 | bytes 5120 | tf_op jit(solution)/shard_map/psum | solution.py:77
  43.3 1.9 scatter_custom_fusion
  45.4 52.0 %all_to_all.10 = bf16[8,48,2560]{2,1,0:T(8,128)(2,1)S(1)} all-to-all(bf16[8,48,2560]{2,1,0:T(8,128)(2,1)S(1)} %bitcast.58), channel_id=1, replica_groups=mesh['grp'=2,'seq'=8,'tp'=2] {'seq'}, dimensions={0} | all-to-all | bytes 3932160 | tf_op jit(solution)/shard_map/all_to_all | solution.py:91
  97.5 8.8 %fusion.2 = f32[8,48,2048]{2,1,0:T(8,128)} fusion(bf16[8,48,2560]{2,1,0:T(8,128)(2,1)S(1)} %all_to_all.10, bf16[2560,2048]{1,0:T(8,128)(2,1)} %param.22), kind=kOutput, calls=%fused_computation.4 | convolution fusion | flops 4026531840 | bytes 15597568 | tf_op jit(solution)/shard_map/scd,df->scf/dot_general | solution.py:93
  106.3 5.9 %fusion.4 = f32[8,48,2048]{2,1,0:T(8,128)} fusion(bf16[8,48,2560]{2,1,0:T(8,128)(2,1)S(1)} %all_to_all.10, bf16[2560,2048]{1,0:T(8,128)(2,1)S(1)} %bitcast.66), kind=kOutput, calls=%fused_computation.6 | convolution fusion | flops 4026531840 | bytes 15597568 | tf_op jit(solution)/shard_map/scd,df->scf/dot_general | solution.py:92
  112.2 30.9 %all-reduce.4.cloned.1.call-done = (f32[8,48,2048]{2,1,0:T(8,128)}, f32[8,48,2048]{2,1,0:T(8,128)}) async-done(((f32[8,48,2048]{2,1,0:T(8,128)}, f32[8,48,2048]{2,1,0:T(8,128)}), (f32[8,48,2048]{2,1,0:T(8,128)}, f32[8,48,2048]{2,1,0:T(8,128)})) %all-reduce.4.cloned.1.call-update) | async-done | bytes 6291472 | tf_op jit(solution)/shard_map/psum | solution.py:94
  143.1 11.4 %fusion.8 = bf16[8,48,2560]{2,1,0:T(8,128)(2,1)} fusion(bf16[2048,2560]{1,0:T(8,128)(2,1)} %param.23, f32[8,48,2048]{2,1,0:T(8,128)} %get-tuple-element.7, f32[8,48,2048]{2,1,0:T(8,128)} %get-tuple-element.8), kind=kOutput, calls=%fused_computation.12 | convolution fusion | flops 4032233472 | bytes 18743296 | tf_op jit(solution)/shard_map/scf,fd->scd/dot_general | solution.py:96
  154.5 5.8 %all-to-all-start.1 = ((bf16[8,48,2560]{2,1,0:T(8,128)(2,1)}), bf16[8,48,2560]{2,1,0:T(8,128)(2,1)}, u32[]{:S(2)}, u32[]{:S(2)}) async-start(bf16[8,48,2560]{2,1,0:T(8,128)(2,1)} %fusion.8), calls=%async_computation.1 | async-start | bytes 3932160 | tf_op jit(solution)/shard_map/all_to_all | solution.py:99
  160.3 46.0 %all-to-all-done.1 = bf16[8,48,2560]{2,1,0:T(8,128)(2,1)} async-done(((bf16[8,48,2560]{2,1,0:T(8,128)(2,1)}), bf16[8,48,2560]{2,1,0:T(8,128)(2,1)}, u32[]{:S(2)}, u32[]{:S(2)}) %all-to-all-start.1) | async-done | bytes 1966112 | tf_op jit(solution)/shard_map/all_to_all | solution.py:99
  206.3 2.2 convert_reduce_fusion
  208.5 2.1 gather_fusion
  210.6 2.3 %fusion.24 = bf16[128,2560]{1,0:T(8,128)(2,1)} fusion(f32[128,2560]{1,0:T(8,128)} %gather_fusion, bf16[128,2560]{1,0:T(8,128)(2,1)S(1)} %get-tuple-element.10), kind=kLoop, calls=%fused_computation.28 | loop fusion | flops 983040 | bytes 2621440 | tf_op jit(solution)/shard_map/convert_element_type | solution.py:104
  (38 shorter events, 3.8 us)
Async XLA Ops:
  6.5 34.0 %copy-start = (bf16[2560,4]{0,1:T(4,128)(2,1)S(1)}, bf16[2560,4]{0,1:T(4,128)(2,1)}, u32[]{:S(2)}) copy-start(bf16[2560,4]{0,1:T(4,128)(2,1)} %param.18) | copy-start | bytes 61444
  6.5 136.6 %all-reduce.4.cloned.1.call-start = ((), (), s32[]{:S(2)}) async-start(), calls=%async_computation.2 | async-start | bytes 12582912 | tf_op jit(solution)/shard_map/psum | solution.py:94
  7.6 8.4 %collective-permute-start.3 = (bf16[128,512]{0,1:T(8,128)(2,1)S(1)}, bf16[128,512]{0,1:T(8,128)(2,1)S(1)}, u32[]{:S(2)}, u32[]{:S(2)}) collective-permute-start(bf16[128,512]{0,1:T(8,128)(2,1)S(1)} %copy.18), channel_id=1, source_target_pairs={{0,2},{2,4},{4,6},{6,8},{8,10},{10,12},{12,14},{1,3},{3,5},{5,7},{... | collective-permute-start | bytes 393224 | tf_op jit(solution)/shard_map/ppermute | solution.py:18
  12.5 7.1 %collective-permute-start = (bf16[128,512]{1,0:T(8,128)(2,1)}, bf16[128,512]{1,0:T(8,128)(2,1)S(1)}, u32[]{:S(2)}, u32[]{:S(2)}) collective-permute-start(bf16[128,512]{1,0:T(8,128)(2,1)} %param.14), channel_id=1, source_target_pairs={{0,2},{2,4},{4,6},{6,8},{8,10},{10,12},{12,14},{1,3},{3,5},{5,7},{... | collective-permute-start | bytes 393224 | tf_op jit(solution)/shard_map/ppermute | solution.py:18
  16.0 8.8 %collective-permute-start.4 = (bf16[128,512]{0,1:T(8,128)(2,1)S(1)}, bf16[128,512]{0,1:T(8,128)(2,1)S(1)}, u32[]{:S(2)}, u32[]{:S(2)}) collective-permute-start(bf16[128,512]{0,1:T(8,128)(2,1)S(1)} %collective-permute-done.3), channel_id=1, source_target_pairs={{0,2},{2,4},{4,6},{6,8},{8,10},{10,12},{12,14},{1,3},{3,5},{5,7},{... | collective-permute-start | bytes 393224 | tf_op jit(solution)/shard_map/ppermute | solution.py:18
  19.6 8.6 %collective-permute-start.1 = (bf16[128,512]{1,0:T(8,128)(2,1)S(1)}, bf16[128,512]{1,0:T(8,128)(2,1)S(1)}, u32[]{:S(2)}, u32[]{:S(2)}) collective-permute-start(bf16[128,512]{1,0:T(8,128)(2,1)S(1)} %collective-permute-done), channel_id=1, source_target_pairs={{0,2},{2,4},{4,6},{6,8},{8,10},{10,12},{12,14},{1,3},{3,5},{5,7},{... | collective-permute-start | bytes 393224 | tf_op jit(solution)/shard_map/ppermute | solution.py:18
  24.8 11.4 %collective-permute-start.5 = (bf16[128,512]{0,1:T(8,128)(2,1)S(1)}, bf16[128,512]{0,1:T(8,128)(2,1)S(1)}, u32[]{:S(2)}, u32[]{:S(2)}) collective-permute-start(bf16[128,512]{0,1:T(8,128)(2,1)S(1)} %collective-permute-done.4), channel_id=1, source_target_pairs={{0,2},{2,4},{4,6},{6,8},{8,10},{10,12},{12,14},{1,3},{3,5},{5,7},{... | collective-permute-start | bytes 393224 | tf_op jit(solution)/shard_map/ppermute | solution.py:18
  28.2 6.9 %collective-permute-start.2 = (bf16[128,512]{1,0:T(8,128)(2,1)S(1)}, bf16[128,512]{1,0:T(8,128)(2,1)S(1)}, u32[]{:S(2)}, u32[]{:S(2)}) collective-permute-start(bf16[128,512]{1,0:T(8,128)(2,1)S(1)} %collective-permute-done.1), channel_id=1, source_target_pairs={{0,2},{2,4},{4,6},{6,8},{8,10},{10,12},{12,14},{1,3},{3,5},{5,7},{... | collective-permute-start | bytes 393224 | tf_op jit(solution)/shard_map/ppermute | solution.py:18
  38.3 1.9 copy-start.2
  39.8 3.5 %copy-start.3 = (s32[128]{0:T(128)S(1)}, s32[128]{0:T(128)}, u32[]{:S(2)}) copy-start(s32[128]{0:T(128)} %param.19) | copy-start | bytes 1540
  45.4 60.9 %slice-start = ((s8[10485760]{0:T(1024)(128)(4,1)}), s8[4194304]{0:T(1024)(128)(4,1)S(1)}, s32[]{:S(2)}) async-start(s8[10485760]{0:T(1024)(128)(4,1)} %bitcast.65), calls=%async_computation.3 | async-start | bytes 8388608
  97.5 8.8 %slice-start.1 = ((s8[10485760]{0:T(1024)(128)(4,1)}), s8[4194304]{0:T(1024)(128)(4,1)S(1)}, s32[]{:S(2)}) async-start(s8[10485760]{0:T(1024)(128)(4,1)} %bitcast.65), calls=%async_computation.4 | async-start | bytes 8388608
  97.5 8.8 %slice-start.2 = ((s8[10485760]{0:T(1024)(128)(4,1)}), s8[2097152]{0:T(1024)(128)(4,1)S(1)}, s32[]{:S(2)}) async-start(s8[10485760]{0:T(1024)(128)(4,1)} %bitcast.65), calls=%async_computation.5 | async-start | bytes 4194304
  154.5 51.8 %all-to-all-start.1 = ((bf16[8,48,2560]{2,1,0:T(8,128)(2,1)}), bf16[8,48,2560]{2,1,0:T(8,128)(2,1)}, u32[]{:S(2)}, u32[]{:S(2)}) async-start(bf16[8,48,2560]{2,1,0:T(8,128)(2,1)} %fusion.8), calls=%async_computation.1 | async-start | bytes 3932160 | tf_op jit(solution)/shard_map/all_to_all | solution.py:99
  208.4 4.4 %copy-start.1 = (bf16[2560,4]{0,1:T(4,128)(2,1)S(1)}, bf16[2560,4]{0,1:T(4,128)(2,1)}, u32[]{:S(2)}) copy-start(bf16[2560,4]{0,1:T(4,128)(2,1)} %param.18) | copy-start | bytes 61444
Sparse Core Ops, SparseCore 0:
  112.3 30.7 all-reduce.3
where the time goes:
time: 220 us
  waiting for transfers between devices  76.9 us (35%)
  blocking collectives  54.5 us (25%)
  starting transfers between devices  29.5 us (13%)
  matrix products  28.8 us (13%)
  between operations  13.7 us (6%)
  other arithmetic  11 us (5%)
  local copies, waits for them, and re-layouts  5.35 us (2%)
    all_to_all x1, blocking collectives, on_device(): lax.all_to_all(outgoing, 'seq', split_axis=0, concat_axis=0, tiled=True)  52 us
    all_to_all x1, waiting for transfers between devices, on_device(): lax.all_to_all(produced, 'seq', split_axis=0, concat_axis=0, tiled=True)  46 us
    psum x1, waiting for transfers between devices, on_device(): gate_full, up_full = lax.psum((gate_part, up_part), 'tp')  30.9 us
    ppermute x6, starting transfers between devices, shifted(): return lax.ppermute(array, axis, pairs)  23.7 us
    dot_general x1, matrix products, on_device(): jnp.einsum('scf,fd->scd', activated, down_weight, preferred_element_type=...  11.4 us
    dot_general x1, matrix products, on_device(): jnp.einsum('scd,df->scf', arrived, up_weight, preferred_element_type=jnp....  8.82 us
    dot_general x1, matrix products, on_device(): jnp.einsum('scd,df->scf', arrived, gate_weight, preferred_element_type=jn...  5.86 us
    all_to_all x1, starting transfers between devices, on_device(): lax.all_to_all(produced, 'seq', split_axis=0, concat_axis=0, tiled=True)  5.77 us
  transfers between devices with their start and end apart: 8, of which 2 were waited for; matrix products, arithmetic and copies ran while one was open for 2% of the time, Pallas kernels for 0%

commit v1 on v0

--- a/solution.py
+++ b/solution.py
@@ -1,8 +1,11 @@
+import functools
 import math
 
 import jax
 import jax.numpy as jnp
 from jax import lax
+from jax.experimental import pallas as pl
+from jax.experimental.pallas import tpu as pltpu
 from jax.sharding import PartitionSpec as P
 
 D = 5120
@@ -16,6 +19,305 @@
     devices = lax.axis_size(axis)
     pairs = [(i, i + by) for i in range(devices) if 0 <= i + by < devices]
     return lax.ppermute(array, axis, pairs)
+
+
+MESH = pl.DeviceIdType.MESH
+VMEM_LIMIT = 60 * 1024 * 1024
+
+
+def peer_of(expert, step):
+    if step == 0:
+        return expert
+    if step == 1:
+        return expert + 1 - 2 * (expert % 2)
+    if step == 2:
+        return (expert + 2) % 4
+    return 3 - expert
+
+
+def expert_kernel(
+    span,
+    cap,
+    ein,
+    sel,
+    sel_t,
+    hid,
+    gate_hbm,
+    up_hbm,
+    down_hbm,
+    out,
+    gate_w,
+    up_w,
+    down_w,
+    outgoing,
+    rows_in,
+    own_part,
+    part_send,
+    part_recv,
+    act,
+    piece,
+    piece_recv,
+    back,
+    returned,
+    w_sem,
+    disp_s,
+    disp_r,
+    fwd_s,
+    fwd_r,
+    tp_s,
+    tp_r,
+    y_s,
+    y_r,
+    z_s,
+    z_r,
+):
+    experts = 4
+    me = lax.axis_index("seq")
+    core = lax.axis_index("tp")
+    e = me // span
+    j = me % span
+    feats = ein.shape[1]
+    hidden = gate_w.shape[1]
+    ft = 512
+    ht = min(512, hidden)
+
+    weights = [
+        pltpu.make_async_copy(src, dst, w_sem.at[i])
+        for i, (src, dst) in enumerate(((gate_hbm, gate_w), (up_hbm, up_w), (down_hbm, down_w)))
+    ]
+    for copy in weights:
+        copy.start()
+
+    barrier = pltpu.get_barrier_semaphore()
+    for step in range(1, experts):
+        pl.semaphore_signal(
+            barrier, inc=1, device_id={"seq": peer_of(e, step) * span + j}, device_id_type=MESH
+        )
+    for d in range(1, span):
+        pl.semaphore_signal(
+            barrier, inc=1, device_id={"seq": e * span + (j + d) % span}, device_id_type=MESH
+        )
+    pl.semaphore_signal(barrier, inc=1, device_id={"tp": 1 - core}, device_id_type=MESH)
+
+    def slots(number):
+        return pl.ds(pl.multiple_of(number * cap, 16), cap)
+
+    @pl.loop(0, feats // ft)
+    def _(c):
+        cols = pl.ds(pl.multiple_of(c * ft, ft), ft)
+        outgoing[:, cols] = jnp.dot(
+            sel[...], ein[:, cols], preferred_element_type=jnp.float32
+        ).astype(jnp.bfloat16)
+
+    pl.semaphore_wait(barrier, experts - 1 + span)
+
+    def disp(step):
+        return pltpu.make_async_remote_copy(
+            src_ref=outgoing.at[slots(peer_of(e, step))],
+            dst_ref=rows_in.at[step, slots(j)],
+            send_sem=disp_s.at[step],
+            recv_sem=disp_r.at[step],
+            device_id={"seq": peer_of(e, step) * span + j},
+            device_id_type=MESH,
+        )
+
+    def fwd(step, d):
+        src = outgoing.at[slots(e)] if step == 0 else rows_in.at[step, slots(j)]
+        return pltpu.make_async_remote_copy(
+            src_ref=src,
+            dst_ref=rows_in.at[step, slots(j)],
+            send_sem=fwd_s.at[step, d],
+            recv_sem=fwd_r.at[step, d],
+            device_id={"seq": e * span + (j + d) % span},
+            device_id_type=MESH,
+        )
+
+    def tp_copy(step):
+        return pltpu.make_async_remote_copy(
+            src_ref=part_send.at[step],
+            dst_ref=part_recv.at[step],
+            send_sem=tp_s.at[step],
+            recv_sem=tp_r.at[step],
+            device_id={"tp": 1 - core},
+            device_id_type=MESH,
+        )
+
+    def y_copy(step, d):
+        return pltpu.make_async_remote_copy(
+            src_ref=piece.at[step, slots((j + d) % span)],
+            dst_ref=piece_recv.at[step, d - 1],
+            send_sem=y_s.at[step, d],
+            recv_sem=y_r.at[step, d],
+            device_id={"seq": e * span + (j + d) % span},
+            device_id_type=MESH,
+        )
+
+    def z_copy(step):
+        return pltpu.make_async_remote_copy(
+            src_ref=back.at[step],
+            dst_ref=returned.at[slots(e)],
+            send_sem=z_s.at[step],
+            recv_sem=z_r.at[step],
+            device_id={"seq": peer_of(e, step) * span + j},
+            device_id_type=MESH,
+        )
+
+    def forward(step):
+        if step > 0:
+            disp(step).wait_recv()
+        for d in range(1, span):
+            fwd(step, d).start()
+
+    def gate_up(step):
+        for d in range(1, span):
+            fwd(step, d).wait_recv()
+
+        @pl.loop(0, hidden // ht)
+        def _(c):
+            for weight, base in ((gate_w, 0), (up_w, hidden)):
+                cols = pl.ds(pl.multiple_of(c * ht, ht), ht)
+                to = pl.ds(pl.multiple_of(base + c * ht, ht), ht)
+                part = jnp.dot(
+                    rows_in[step], weight[:, cols], preferred_element_type=jnp.float32
+                )
+                own_part[step, :, to] = part
+                part_send[step, :, to] = part.astype(jnp.bfloat16)
+
+        tp_copy(step).start()
+
+    def down(step):
+        tp_copy(step).wait_recv()
+
+        @pl.loop(0, hidden // ht)
+        def _(c):
+            cols = pl.ds(pl.multiple_of(c * ht, ht), ht)
+            ups = pl.ds(pl.multiple_of(hidden + c * ht, ht), ht)
+            gate = own_part[step, :, cols] + part_recv[step, :, cols].astype(jnp.float32)
+            up = own_part[step, :, ups] + part_recv[step, :, ups].astype(jnp.float32)
+            act[:, cols] = (jax.nn.silu(gate) * up).astype(jnp.bfloat16)
+
+        @pl.loop(0, feats // ft)
+        def _(c):
+            cols = pl.ds(pl.multiple_of(c * ft, ft), ft)
+            piece[step, :, cols] = jnp.dot(
+                act[...], down_w[:, cols], preferred_element_type=jnp.float32
+            ).astype(jnp.bfloat16)
+
+        for d in range(1, span):
+            y_copy(step, d).start()
+
+    def give_back(step):
+        for d in range(1, span):
+            y_copy(step, d).wait_recv()
+
+        @pl.loop(0, feats // ft)
+        def _(c):
+            cols = pl.ds(pl.multiple_of(c * ft, ft), ft)
+            total = piece[step, slots(j), cols].astype(jnp.float32)
+            for d in range(1, span):
+                total += piece_recv[step, d - 1, :, cols].astype(jnp.float32)
+            if step == 0:
+                returned[slots(e), cols] = total.astype(jnp.bfloat16)
+            else:
+                back[step, :, cols] = total.astype(jnp.bfloat16)
+
+        if step > 0:
+            z_copy(step).start()
+
+    for step in (3, 2, 1):
+        disp(step).start()
+    forward(0)
+    rows_in[0, slots(j)] = outgoing[slots(e)]
+    forward(1)
+    weights[0].wait()
+    weights[1].wait()
+    gate_up(0)
+    forward(2)
+    gate_up(1)
+    forward(3)
+    weights[2].wait()
+    down(0)
+    down(1)
+    gate_up(2)
+    give_back(1)
+    gate_up(3)
+    down(2)
+    give_back(0)
+    down(3)
+    give_back(2)
+    give_back(3)
+    for step in range(1, experts):
+        z_copy(step).wait_recv()
+
+    @pl.loop(0, feats // ft)
+    def _(c):
+        cols = pl.ds(pl.multiple_of(c * ft, ft), ft)
+        picked = jnp.dot(sel_t[...], returned[:, cols], preferred_element_type=jnp.float32)
+        out[:, cols] = (hid[:, cols].astype(jnp.float32) + picked).astype(jnp.bfloat16)
+
+    for step in range(experts):
+        if step > 0:
+            disp(step).wait_send()
+            z_copy(step).wait_send()
+        tp_copy(step).wait_send()
+        for d in range(1, span):
+            fwd(step, d).wait_send()
+            y_copy(step, d).wait_send()
+
+
+def expert_block(expert_in, select, hidden_state, gate_weight, up_weight, down_weight, cap, span):
+    tokens, feats = expert_in.shape
+    hidden = gate_weight.shape[1]
+    experts = select.shape[0] // cap
+    rows = span * cap
+    bf16 = jnp.bfloat16
+    vmem = pl.BlockSpec(memory_space=pltpu.VMEM)
+    hbm = pl.BlockSpec(memory_space=pl.ANY)
+    dma = pltpu.SemaphoreType.DMA
+    return pl.pallas_call(
+        functools.partial(expert_kernel, span, cap),
+        out_shape=jax.ShapeDtypeStruct((tokens, feats), bf16),
+        in_specs=[vmem] * 4 + [hbm] * 3,
+        out_specs=vmem,
+        scratch_shapes=[
+            pltpu.VMEM((feats, hidden), bf16),
+            pltpu.VMEM((feats, hidden), bf16),
+            pltpu.VMEM((hidden, feats), bf16),
+            pltpu.VMEM((experts * cap, feats), bf16),
+            pltpu.VMEM((experts, rows, feats), bf16),
+            pltpu.VMEM((experts, rows, 2 * hidden), jnp.float32),
+            pltpu.VMEM((experts, rows, 2 * hidden), bf16),
+            pltpu.VMEM((experts, rows, 2 * hidden), bf16),
+            pltpu.VMEM((rows, hidden), bf16),
+            pltpu.VMEM((experts, rows, feats), bf16),
+            pltpu.VMEM((experts, span - 1, cap, feats), bf16),
+            pltpu.VMEM((experts, cap, feats), bf16),
+            pltpu.VMEM((experts * cap, feats), bf16),
+            dma((3,)),
+            dma((experts,)),
+            dma((experts,)),
+            dma((experts, span)),
+            dma((experts, span)),
+            dma((experts,)),
+            dma((experts,)),
+            dma((experts, span)),
+            dma((experts, span)),
+            dma((experts,)),
+            dma((experts,)),
+        ],
+        compiler_params=pltpu.CompilerParams(
+            collective_id=0, has_side_effects=True, vmem_limit_bytes=VMEM_LIMIT
+        ),
+        name="experts",
+    )(
+        expert_in,
+        select,
+        select.T,
+        hidden_state,
+        gate_weight,
+        up_weight,
+        down_weight,
+    )
 
 
 def on_device(
@@ -83,25 +385,20 @@
     expert_in = (gained.astype(jnp.float32) * factor[:, None]).astype(jnp.bfloat16)
     capacity = 3 * tokens_dev // (2 * experts_all)
     slices_per_expert = lax.axis_size("seq") // experts_all
-    features = expert_in.shape[1]
     place = expert_id * capacity + slot_index
-    buffer = jnp.zeros((experts_all * capacity, features), jnp.bfloat16).at[place].set(expert_in)
-    buffer = buffer.reshape(experts_all, capacity, features)
-    outgoing = jnp.repeat(buffer, slices_per_expert, axis=0)
-    arrived = lax.all_to_all(outgoing, "seq", split_axis=0, concat_axis=0, tiled=True)
-    gate_part = jnp.einsum("scd,df->scf", arrived, gate_weight, preferred_element_type=jnp.float32)
-    up_part = jnp.einsum("scd,df->scf", arrived, up_weight, preferred_element_type=jnp.float32)
-    gate_full, up_full = lax.psum((gate_part, up_part), "tp")
-    activated = (jax.nn.silu(gate_full) * up_full).astype(jnp.bfloat16)
-    produced = jnp.einsum(
-        "scf,fd->scd", activated, down_weight, preferred_element_type=jnp.float32
+    select = (
+        jnp.arange(experts_all * capacity, dtype=jnp.int32)[:, None] == place[None, :]
     ).astype(jnp.bfloat16)
-    returned = lax.all_to_all(produced, "seq", split_axis=0, concat_axis=0, tiled=True)
-    summed = jnp.sum(
-        returned.reshape(experts_all, slices_per_expert, capacity, -1).astype(jnp.float32), axis=1
-    )
-    expert_out = summed.reshape(experts_all * capacity, -1)[place]
-    return (hidden_state.astype(jnp.float32) + expert_out).astype(jnp.bfloat16)
+    return expert_block(
+        expert_in,
+        select,
+        hidden_state,
+        gate_weight,
+        up_weight,
+        down_weight,
+        capacity,
+        slices_per_expert,
+    )
 
 
 def solution(mesh):

time: 220 us -> 124 us (0.56)
  Pallas kernels: 0 us -> 82.3 us
  waiting for transfers between devices: 76.9 us -> 0.02 us
  blocking collectives: 54.5 us -> 2.46 us
  matrix products: 28.8 us -> 2.7 us
  between operations: 13.7 us -> 0.22 us
  starting transfers between devices: 29.5 us -> 22.2 us
  other arithmetic: 11 us -> 7.03 us
    pallas_call x0 -> x1, Pallas kernels: none -> 82.3 us  [expert_block(): pl.pallas_call(functools.partial(expert_kernel, span, cap), out_shape=jax...]
    all_to_all x1 -> x0, blocking collectives: 52 us -> none  [on_device(): lax.all_to_all(outgoing, 'seq', split_axis=0, concat_axis=0, tiled=True)]
    all_to_all x1 -> x0, waiting for transfers between devices: 46 us -> none  [on_device(): lax.all_to_all(produced, 'seq', split_axis=0, concat_axis=0, tiled=True)]
    psum x1 -> x0, waiting for transfers between devices: 30.9 us -> none  [on_device(): gate_full, up_full = lax.psum((gate_part, up_part), 'tp')]
    dot_general x3 -> x0, matrix products: 26.1 us -> none  [the longest x1 11.4 us: on_device(): jnp.einsum('scf,fd->scd', activated, down_weight, preferred_element_type=...]
    all_to_all x1 -> x0, starting transfers between devices: 5.77 us -> none  [on_device(): lax.all_to_all(produced, 'seq', split_axis=0, concat_axis=0, tiled=True)]
    unnamed x16 -> x11, local copies, waits for them, and re-layouts: 2.47 us -> 4.42 us
  transfers between devices with their start and end apart: 8 -> 6, of which waited for: 2 -> 0; matrix products, arithmetic and copies ran while one was open for 2% -> 5% of each run, Pallas kernels for 0% -> 0%
where the time goes in v1:
time: 124 us; the launch traced here: 122 us
  Pallas kernels  82.3 us (66%)
  starting transfers between devices  22.2 us (18%)
  other arithmetic  7.03 us (6%)
  local copies, waits for them, and re-layouts  5.03 us (4%)
  matrix products  2.7 us (2%)
  blocking collectives  2.46 us (2%)
    pallas_call x1, Pallas kernels, expert_block(): pl.pallas_call(functools.partial(expert_kernel, span, cap), out_shape=jax...  82.3 us
    ppermute x6, starting transfers between devices, shifted(): return lax.ppermute(array, axis, pairs)  22.2 us
    unnamed x11, local copies, waits for them, and re-layouts  4.42 us
  transfers between devices with their start and end apart: 6, of which 0 were waited for; matrix products, arithmetic and copies ran while one was open for 5% of the time, Pallas kernels for 0%

profile of v1, /device:TPU:0, one launch (start us, length us, event | category | flops | bytes accessed | tf_op | source)
XLA Modules:
  0.0 121.9 jit_solution(342622166124781045)
XLA Ops:
  0.0 1.0 copy.18
  1.0 4.9 %collective-permute-start.3 = (bf16[128,512]{0,1:T(8,128)(2,1)S(1)}, bf16[128,512]{0,1:T(8,128)(2,1)S(1)}, u32[]{:S(2)}, u32[]{:S(2)}) collective-permute-start(bf16[128,512]{0,1:T(8,128)(2,1)S(1)} %copy.18), channel_id=1, source_target_pairs={{0,2},{2,4},{4,6},{6,8},{8,10},{10,12},{12,14},{1,3},{3,5},{5,7},{... | collective-permute-start | bytes 393224 | tf_op jit(solution)/shard_map/ppermute | solution.py:21
  5.9 3.4 %collective-permute-start = (bf16[128,512]{1,0:T(8,128)(2,1)}, bf16[128,512]{1,0:T(8,128)(2,1)S(1)}, u32[]{:S(2)}, u32[]{:S(2)}) collective-permute-start(bf16[128,512]{1,0:T(8,128)(2,1)} %param.14), channel_id=1, source_target_pairs={{0,2},{2,4},{4,6},{6,8},{8,10},{10,12},{12,14},{1,3},{3,5},{5,7},{... | collective-permute-start | bytes 393224 | tf_op jit(solution)/shard_map/ppermute | solution.py:21
  9.4 0.9 compare_and_fusion
  10.3 0.7 multiply_add_fusion
  10.9 3.4 %collective-permute-start.4 = (bf16[128,512]{0,1:T(8,128)(2,1)S(1)}, bf16[128,512]{0,1:T(8,128)(2,1)S(1)}, u32[]{:S(2)}, u32[]{:S(2)}) collective-permute-start(bf16[128,512]{0,1:T(8,128)(2,1)S(1)} %collective-permute-done.3), channel_id=1, source_target_pairs={{0,2},{2,4},{4,6},{6,8},{8,10},{10,12},{12,14},{1,3},{3,5},{5,7},{... | collective-permute-start | bytes 393224 | tf_op jit(solution)/shard_map/ppermute | solution.py:21
  14.4 3.4 %collective-permute-start.1 = (bf16[128,512]{1,0:T(8,128)(2,1)S(1)}, bf16[128,512]{1,0:T(8,128)(2,1)S(1)}, u32[]{:S(2)}, u32[]{:S(2)}) collective-permute-start(bf16[128,512]{1,0:T(8,128)(2,1)S(1)} %collective-permute-done), channel_id=1, source_target_pairs={{0,2},{2,4},{4,6},{6,8},{8,10},{10,12},{12,14},{1,3},{3,5},{5,7},{... | collective-permute-start | bytes 393224 | tf_op jit(solution)/shard_map/ppermute | solution.py:21
  17.8 0.7 fusion.19.sel_t
  18.5 3.4 %collective-permute-start.5 = (bf16[128,512]{0,1:T(8,128)(2,1)S(1)}, bf16[128,512]{0,1:T(8,128)(2,1)S(1)}, u32[]{:S(2)}, u32[]{:S(2)}) collective-permute-start(bf16[128,512]{0,1:T(8,128)(2,1)S(1)} %collective-permute-done.4), channel_id=1, source_target_pairs={{0,2},{2,4},{4,6},{6,8},{8,10},{10,12},{12,14},{1,3},{3,5},{5,7},{... | collective-permute-start | bytes 393224 | tf_op jit(solution)/shard_map/ppermute | solution.py:21
  22.0 3.6 %collective-permute-start.2 = (bf16[128,512]{1,0:T(8,128)(2,1)S(1)}, bf16[128,512]{1,0:T(8,128)(2,1)S(1)}, u32[]{:S(2)}, u32[]{:S(2)}) collective-permute-start(bf16[128,512]{1,0:T(8,128)(2,1)S(1)} %collective-permute-done.1), channel_id=1, source_target_pairs={{0,2},{2,4},{4,6},{6,8},{8,10},{10,12},{12,14},{1,3},{3,5},{5,7},{... | collective-permute-start | bytes 393224 | tf_op jit(solution)/shard_map/ppermute | solution.py:21
  25.6 0.6 fusion.20.sel
  26.2 1.4 %copy.20 = bf16[128,2560]{0,1:T(8,128)(2,1)S(1)} copy(bf16[128,2560]{1,0:T(8,128)(2,1)} %param.12) | data formatting | bytes 1310720 | tf_op args[0]
  27.6 0.7 convert_element_type.34
  28.3 0.9 pad_maximum_fusion
  29.6 0.9 fusion.2
  30.5 1.1 fusion
  31.6 1.5 %fusion.14 = f32[128,4,5,128]{0,3,2,1:T(8,128)S(1)} fusion(bf16[512,4,128,1]{0,2,3,1:T(8,128)(2,1)S(1)} %bitcast.41, f32[4,512,128,5]{2,1,3,0:T(8,128)S(1)} %get-tuple-element.10, f32[4,5,128]{2,1,0:T(8,128)S(1)} %get-tuple-element.9, pred[128,512]{0,1:T(8,128)(4,1)S(1)} %compare_and_fusion, f32[128,4,5]{0,2,1:T(8,128)S(1)} %bitcast.42), kind=kOutput, calls=%fused_computation.17 | convolution fusion | flops 341114880 | bytes 7163904 | tf_op jit(solution)/shard_map/kgts,skd->tkgd/dot_general | solution.py:371
  33.1 0.4 copy.24
  33.5 0.3 fusion.13
  33.8 0.3 fusion.17
  34.1 2.5 %all-reduce = (f32[128,4]{0,1:T(4,128)S(1)}, f32[128]{0:T(128)S(1)}) all-reduce(f32[128,4]{0,1:T(4,128)S(1)} %fusion.17, f32[128]{0:T(128)S(1)} %get-tuple-element.7), channel_id=1, replica_groups=mesh['grp'=2,'seq'=8,'tp'=2] {'tp'}, use_global_device_ids=true, to_apply=%region_4.5 | all-reduce | flops 640 | bytes 5120 | tf_op jit(solution)/shard_map/psum | solution.py:379
  36.6 1.1 multiply_convert_fusion.ein
  37.6 82.3 %experts.1 = bf16[128,2560]{1,0:T(8,128)(2,1)} custom-call(bf16[128,2560]{1,0:T(8,128)(2,1)} %multiply_convert_fusion.ein, bf16[192,128]{1,0:T(8,128)(2,1)} %fusion.20.sel, bf16[128,192]{1,0:T(8,128)(2,1)} %fusion.19.sel_t, bf16[128,2560]{1,0:T(8,128)(2,1)} %copy-done.1, bf16[2560,2048]{1,0:T(8,128)(2,1)} %gate_hbm.1, bf16[2560,2048]{1,0:T(8,128)(2,1)} %up_hbm.1, ...), custom_call_target="tpu_custom_call" | custom-call | tf_op jit(solution)/shard_map/experts/pallas_call | solution.py:277
  120.0 2.0 %copy.32 = bf16[128,2560]{1,0:T(8,128)(2,1)} copy(bf16[128,2560]{1,0:T(8,128)(2,1)} %experts.1) | data formatting | bytes 1310720
  (21 shorter events, 0.4 us)
Async XLA Ops:
  0.0 33.8 %copy-start = (bf16[2560,4]{0,1:T(4,128)(2,1)S(1)}, bf16[2560,4]{0,1:T(4,128)(2,1)}, u32[]{:S(2)}) copy-start(bf16[2560,4]{0,1:T(4,128)(2,1)} %param.18) | copy-start | bytes 61444
  1.0 9.9 %collective-permute-start.3 = (bf16[128,512]{0,1:T(8,128)(2,1)S(1)}, bf16[128,512]{0,1:T(8,128)(2,1)S(1)}, u32[]{:S(2)}, u32[]{:S(2)}) collective-permute-start(bf16[128,512]{0,1:T(8,128)(2,1)S(1)} %copy.18), channel_id=1, source_target_pairs={{0,2},{2,4},{4,6},{6,8},{8,10},{10,12},{12,14},{1,3},{3,5},{5,7},{... | collective-permute-start | bytes 393224 | tf_op jit(solution)/shard_map/ppermute | solution.py:21
  5.9 8.5 %collective-permute-start = (bf16[128,512]{1,0:T(8,128)(2,1)}, bf16[128,512]{1,0:T(8,128)(2,1)S(1)}, u32[]{:S(2)}, u32[]{:S(2)}) collective-permute-start(bf16[128,512]{1,0:T(8,128)(2,1)} %param.14), channel_id=1, source_target_pairs={{0,2},{2,4},{4,6},{6,8},{8,10},{10,12},{12,14},{1,3},{3,5},{5,7},{... | collective-permute-start | bytes 393224 | tf_op jit(solution)/shard_map/ppermute | solution.py:21
  10.9 7.6 %collective-permute-start.4 = (bf16[128,512]{0,1:T(8,128)(2,1)S(1)}, bf16[128,512]{0,1:T(8,128)(2,1)S(1)}, u32[]{:S(2)}, u32[]{:S(2)}) collective-permute-start(bf16[128,512]{0,1:T(8,128)(2,1)S(1)} %collective-permute-done.3), channel_id=1, source_target_pairs={{0,2},{2,4},{4,6},{6,8},{8,10},{10,12},{12,14},{1,3},{3,5},{5,7},{... | collective-permute-start | bytes 393224 | tf_op jit(solution)/shard_map/ppermute | solution.py:21
  14.4 7.6 %collective-permute-start.1 = (bf16[128,512]{1,0:T(8,128)(2,1)S(1)}, bf16[128,512]{1,0:T(8,128)(2,1)S(1)}, u32[]{:S(2)}, u32[]{:S(2)}) collective-permute-start(bf16[128,512]{1,0:T(8,128)(2,1)S(1)} %collective-permute-done), channel_id=1, source_target_pairs={{0,2},{2,4},{4,6},{6,8},{8,10},{10,12},{12,14},{1,3},{3,5},{5,7},{... | collective-permute-start | bytes 393224 | tf_op jit(solution)/shard_map/ppermute | solution.py:21
  18.5 10.9 %collective-permute-start.5 = (bf16[128,512]{0,1:T(8,128)(2,1)S(1)}, bf16[128,512]{0,1:T(8,128)(2,1)S(1)}, u32[]{:S(2)}, u32[]{:S(2)}) collective-permute-start(bf16[128,512]{0,1:T(8,128)(2,1)S(1)} %collective-permute-done.4), channel_id=1, source_target_pairs={{0,2},{2,4},{4,6},{6,8},{8,10},{10,12},{12,14},{1,3},{3,5},{5,7},{... | collective-permute-start | bytes 393224 | tf_op jit(solution)/shard_map/ppermute | solution.py:21
  22.0 6.3 %collective-permute-start.2 = (bf16[128,512]{1,0:T(8,128)(2,1)S(1)}, bf16[128,512]{1,0:T(8,128)(2,1)S(1)}, u32[]{:S(2)}, u32[]{:S(2)}) collective-permute-start(bf16[128,512]{1,0:T(8,128)(2,1)S(1)} %collective-permute-done.1), channel_id=1, source_target_pairs={{0,2},{2,4},{4,6},{6,8},{8,10},{10,12},{12,14},{1,3},{3,5},{5,7},{... | collective-permute-start | bytes 393224 | tf_op jit(solution)/shard_map/ppermute | solution.py:21
  31.6 1.9 %copy-start.2 = (bf16[128,2560]{1,0:T(8,128)(2,1)S(1)}, bf16[128,2560]{1,0:T(8,128)(2,1)}, u32[]{:S(2)}) copy-start(bf16[128,2560]{1,0:T(8,128)(2,1)} %param.15) | copy-start | bytes 1966084
  33.1 3.5 %copy-start.3 = (s32[128]{0:T(128)S(1)}, s32[128]{0:T(128)}, u32[]{:S(2)}) copy-start(s32[128]{0:T(128)} %param.19) | copy-start | bytes 1540
  33.8 3.9 %copy-start.1 = (bf16[128,2560]{1,0:T(8,128)(2,1)}, bf16[128,2560]{1,0:T(8,128)(2,1)S(1)}, u32[]{:S(2)}) copy-start(bf16[128,2560]{1,0:T(8,128)(2,1)S(1)} %get-tuple-element.8.hid) | copy-start | bytes 1966084

commit v2 on v1

--- a/solution.py
+++ b/solution.py
@@ -13,12 +13,6 @@
 KVH = 8
 HD = 128
 STRETCH_DEVS = 4
-
-
-def shifted(array, axis, by):
-    devices = lax.axis_size(axis)
-    pairs = [(i, i + by) for i in range(devices) if 0 <= i + by < devices]
-    return lax.ppermute(array, axis, pairs)
 
 
 MESH = pl.DeviceIdType.MESH
@@ -35,13 +29,16 @@
     return 3 - expert
 
 
-def expert_kernel(
+def layer_kernel(
     span,
     cap,
-    ein,
-    sel,
-    sel_t,
-    hid,
+    queries,
+    keys,
+    values,
+    residual,
+    ids,
+    gain,
+    router,
     gate_hbm,
     up_hbm,
     down_hbm,
@@ -49,6 +46,15 @@
     gate_w,
     up_w,
     down_w,
+    key_all,
+    value_all,
+    bias,
+    probs,
+    totals,
+    hid,
+    gained,
+    stat,
+    stat_recv,
     outgoing,
     rows_in,
     own_part,
@@ -60,6 +66,12 @@
     back,
     returned,
     w_sem,
+    k_s,
+    k_r,
+    v_s,
+    v_r,
+    st_s,
+    st_r,
     disp_s,
     disp_r,
     fwd_s,
@@ -76,7 +88,8 @@
     core = lax.axis_index("tp")
     e = me // span
     j = me % span
-    feats = ein.shape[1]
+    feats = queries.shape[1]
+    tokens = queries.shape[0]
     hidden = gate_w.shape[1]
     ft = 512
     ht = min(512, hidden)
@@ -98,18 +111,146 @@
             barrier, inc=1, device_id={"seq": e * span + (j + d) % span}, device_id_type=MESH
         )
     pl.semaphore_signal(barrier, inc=1, device_id={"tp": 1 - core}, device_id_type=MESH)
+    place = me % STRETCH_DEVS
+    for d in range(1, STRETCH_DEVS):
+        pl.semaphore_signal(
+            barrier,
+            inc=1,
+            device_id={"seq": me - place + (place + d) % STRETCH_DEVS},
+            device_id_type=MESH,
+        )
 
     def slots(number):
         return pl.ds(pl.multiple_of(number * cap, 16), cap)
+
+    f32 = jnp.float32
+    key_all[0] = keys[...]
+    value_all[0] = values[...]
+
+    across = lax.broadcasted_iota(jnp.int32, (tokens, tokens), 1)
+    below = lax.broadcasted_iota(jnp.int32, (tokens, tokens), 0)
+
+    def column(row):
+        spread = jnp.broadcast_to(ids[row : row + 1, :].astype(f32), (tokens, tokens))
+        return jnp.sum(jnp.where(across == below, spread, 0.0), axis=1, keepdims=True).astype(
+            jnp.int32
+        )
+
+    start_col = column(0)
+    expert_col = column(1)
+    place_col = column(2)
+    query_pos = me * tokens + below
+    for d in range(STRETCH_DEVS):
+        key_pos = (me - d) * tokens + across
+        allowed = (
+            (key_pos <= query_pos) & (key_pos >= start_col) & (key_pos >= (me - place) * tokens)
+        )
+        bias[:, d * tokens : (d + 1) * tokens] = jnp.where(allowed, 0.0, -jnp.inf)
+
+    pl.semaphore_wait(barrier, experts - 1 + span + STRETCH_DEVS - 1)
+
+    def kv_copy(src, dst, send, recv, d):
+        return pltpu.make_async_remote_copy(
+            src_ref=src,
+            dst_ref=dst.at[d],
+            send_sem=send.at[d],
+            recv_sem=recv.at[d],
+            device_id={"seq": me + d},
+            device_id_type=MESH,
+        )
+
+    for src, dst, send, recv in (
+        (keys, key_all, k_s, k_r),
+        (values, value_all, v_s, v_r),
+    ):
+        for d in range(STRETCH_DEVS - 1, 0, -1):
+
+            @pl.when(place + d < STRETCH_DEVS)
+            def _():
+                kv_copy(src, dst, send, recv, d).start()
+
+            @pl.when(place < d)
+            def _():
+                dst[d] = jnp.zeros_like(src)
+
+    for d in range(1, STRETCH_DEVS):
+
+        @pl.when(place >= d)
+        def _():
+            kv_copy(keys, key_all, k_s, k_r, d).wait_recv()
+
+    kv_heads = keys.shape[1] // HD
+    per_group = QH // KVH
+    scale = math.log2(math.e) / math.sqrt(HD)
+
+    @pl.loop(0, kv_heads)
+    def _(g):
+        kcols = pl.ds(pl.multiple_of(g * HD, HD), HD)
+        key_block = key_all[:, :, kcols].reshape(STRETCH_DEVS * tokens, HD)
+        for r in range(per_group):
+            h = g * per_group + r
+            cols = pl.ds(pl.multiple_of(h * HD, HD), HD)
+            scores = lax.dot_general(
+                queries[:, cols], key_block, (((1,), (1,)), ((), ())), preferred_element_type=f32
+            )
+            masked = scores + bias[...]
+            largest = jnp.max(masked, axis=1, keepdims=True)
+            expo = jnp.exp2((masked - largest) * scale)
+            totals[h] = jnp.broadcast_to(jnp.sum(expo, axis=1, keepdims=True), (tokens, HD))
+            probs[h] = expo.astype(jnp.bfloat16)
+
+    for d in range(1, STRETCH_DEVS):
+
+        @pl.when(place >= d)
+        def _():
+            kv_copy(values, value_all, v_s, v_r, d).wait_recv()
+
+    stat[...] = jnp.zeros_like(stat)
+
+    @pl.loop(0, kv_heads)
+    def _(g):
+        kcols = pl.ds(pl.multiple_of(g * HD, HD), HD)
+        value_block = value_all[:, :, kcols].reshape(STRETCH_DEVS * tokens, HD)
+        for r in range(per_group):
+            h = g * per_group + r
+            cols = pl.ds(pl.multiple_of(h * HD, HD), HD)
+            attended = jnp.dot(probs[h], value_block, preferred_element_type=f32) / totals[h]
+            state = (residual[:, cols].astype(f32) + attended).astype(jnp.bfloat16)
+            hid[:, cols] = state
+            wide = state.astype(f32)
+            gained[:, cols] = (wide * gain[:, cols].astype(f32)).astype(jnp.bfloat16)
+            stat[...] += wide * wide
+
+    square = jnp.sum(stat[...], axis=1, keepdims=True)
+    logits = jnp.dot(gained[...], router[...], preferred_element_type=f32)
+    lane = lax.broadcasted_iota(jnp.int32, (tokens, experts), 1)
+    picked = jnp.sum(jnp.where(lane == expert_col, logits, 0.0), axis=1, keepdims=True)
+    stat[...] = jnp.where(across == 0, picked, square)
+    stat_copy = pltpu.make_async_remote_copy(
+        src_ref=stat,
+        dst_ref=stat_recv,
+        send_sem=st_s.at[0],
+        recv_sem=st_r.at[0],
+        device_id={"tp": 1 - core},
+        device_id_type=MESH,
+    )
+    stat_copy.start()
+    slot_row = lax.broadcasted_iota(jnp.int32, (experts * cap, tokens), 0)
+    slot_lane = lax.broadcasted_iota(jnp.int32, (tokens, experts * cap), 1)
+    sel = jnp.where(slot_row == ids[2:3, :], 1.0, 0.0).astype(jnp.bfloat16)
+    sel_t = jnp.where(slot_lane == place_col, 1.0, 0.0).astype(jnp.bfloat16)
+    stat_copy.wait_recv()
+    both = stat[...] + stat_recv[...]
+    inverse = lax.rsqrt(both[:, 1:2] / D + 1e-05)
+    factor = inverse * jax.nn.sigmoid(inverse * both[:, 0:1])
 
     @pl.loop(0, feats // ft)
     def _(c):
         cols = pl.ds(pl.multiple_of(c * ft, ft), ft)
-        outgoing[:, cols] = jnp.dot(
-            sel[...], ein[:, cols], preferred_element_type=jnp.float32
-        ).astype(jnp.bfloat16)
-
-    pl.semaphore_wait(barrier, experts - 1 + span)
+        expert_in = (gained[:, cols].astype(f32) * factor).astype(jnp.bfloat16)
+        outgoing[:, cols] = jnp.dot(sel, expert_in, preferred_element_type=f32).astype(
+            jnp.bfloat16
+        )
 
     def disp(step):
         return pltpu.make_async_remote_copy(
@@ -180,7 +321,7 @@
                 part = jnp.dot(
                     rows_in[step], weight[:, cols], preferred_element_type=jnp.float32
                 )
-                own_part[step, :, to] = part
+                own_part[step % 2, :, to] = part
                 part_send[step, :, to] = part.astype(jnp.bfloat16)
 
         tp_copy(step).start()
@@ -192,8 +333,8 @@
         def _(c):
             cols = pl.ds(pl.multiple_of(c * ht, ht), ht)
             ups = pl.ds(pl.multiple_of(hidden + c * ht, ht), ht)
-            gate = own_part[step, :, cols] + part_recv[step, :, cols].astype(jnp.float32)
-            up = own_part[step, :, ups] + part_recv[step, :, ups].astype(jnp.float32)
+            gate = own_part[step % 2, :, cols] + part_recv[step, :, cols].astype(jnp.float32)
+            up = own_part[step % 2, :, ups] + part_recv[step, :, ups].astype(jnp.float32)
             act[:, cols] = (jax.nn.silu(gate) * up).astype(jnp.bfloat16)
 
         @pl.loop(0, feats // ft)
@@ -224,27 +365,28 @@
         if step > 0:
             z_copy(step).start()
 
-    for step in (3, 2, 1):
-        disp(step).start()
+    disp(2).start()
+    disp(1).start()
     forward(0)
     rows_in[0, slots(j)] = outgoing[slots(e)]
-    forward(1)
     weights[0].wait()
     weights[1].wait()
+    forward(1)
     gate_up(0)
+    disp(3).start()
     forward(2)
     gate_up(1)
-    forward(3)
     weights[2].wait()
     down(0)
     down(1)
+    forward(3)
     gate_up(2)
     give_back(1)
+    down(2)
     gate_up(3)
-    down(2)
+    give_back(2)
+    down(3)
     give_back(0)
-    down(3)
-    give_back(2)
     give_back(3)
     for step in range(1, experts):
         z_copy(step).wait_recv()
@@ -252,8 +394,16 @@
     @pl.loop(0, feats // ft)
     def _(c):
         cols = pl.ds(pl.multiple_of(c * ft, ft), ft)
-        picked = jnp.dot(sel_t[...], returned[:, cols], preferred_element_type=jnp.float32)
+        picked = jnp.dot(sel_t, returned[:, cols], preferred_element_type=jnp.float32)
         out[:, cols] = (hid[:, cols].astype(jnp.float32) + picked).astype(jnp.bfloat16)
+
+    stat_copy.wait_send()
+    for d in range(1, STRETCH_DEVS):
+
+        @pl.when(place + d < STRETCH_DEVS)
+        def _():
+            kv_copy(keys, key_all, k_s, k_r, d).wait_send()
+            kv_copy(values, value_all, v_s, v_r, d).wait_send()
 
     for step in range(experts):
         if step > 0:
@@ -265,27 +415,52 @@
             y_copy(step, d).wait_send()
 
 
-def expert_block(expert_in, select, hidden_state, gate_weight, up_weight, down_weight, cap, span):
-    tokens, feats = expert_in.shape
+def on_device(
+    queries,
+    key_heads,
+    values,
+    residual,
+    doc_start,
+    norm_gain,
+    router,
+    expert_id,
+    slot_index,
+    gate_weight,
+    up_weight,
+    down_weight,
+):
+    tokens, feats = queries.shape
     hidden = gate_weight.shape[1]
-    experts = select.shape[0] // cap
+    experts = router.shape[1]
+    cap = 3 * tokens // (2 * experts)
+    span = lax.axis_size("seq") // experts
     rows = span * cap
     bf16 = jnp.bfloat16
+    ids = jnp.stack([doc_start, expert_id, expert_id * cap + slot_index] + [expert_id] * 5)
     vmem = pl.BlockSpec(memory_space=pltpu.VMEM)
     hbm = pl.BlockSpec(memory_space=pl.ANY)
     dma = pltpu.SemaphoreType.DMA
     return pl.pallas_call(
-        functools.partial(expert_kernel, span, cap),
+        functools.partial(layer_kernel, span, cap),
         out_shape=jax.ShapeDtypeStruct((tokens, feats), bf16),
-        in_specs=[vmem] * 4 + [hbm] * 3,
+        in_specs=[vmem] * 7 + [hbm] * 3,
         out_specs=vmem,
         scratch_shapes=[
             pltpu.VMEM((feats, hidden), bf16),
             pltpu.VMEM((feats, hidden), bf16),
             pltpu.VMEM((hidden, feats), bf16),
+            pltpu.VMEM((STRETCH_DEVS, tokens, key_heads.shape[1]), bf16),
+            pltpu.VMEM((STRETCH_DEVS, tokens, key_heads.shape[1]), bf16),
+            pltpu.VMEM((tokens, STRETCH_DEVS * tokens), jnp.float32),
+            pltpu.VMEM((feats // HD, tokens, STRETCH_DEVS * tokens), bf16),
+            pltpu.VMEM((feats // HD, tokens, HD), jnp.float32),
+            pltpu.VMEM((tokens, feats), bf16),
+            pltpu.VMEM((tokens, feats), bf16),
+            pltpu.VMEM((tokens, tokens), jnp.float32),
+            pltpu.VMEM((tokens, tokens), jnp.float32),
             pltpu.VMEM((experts * cap, feats), bf16),
             pltpu.VMEM((experts, rows, feats), bf16),
-            pltpu.VMEM((experts, rows, 2 * hidden), jnp.float32),
+            pltpu.VMEM((2, rows, 2 * hidden), jnp.float32),
             pltpu.VMEM((experts, rows, 2 * hidden), bf16),
             pltpu.VMEM((experts, rows, 2 * hidden), bf16),
             pltpu.VMEM((rows, hidden), bf16),
@@ -294,6 +469,12 @@
             pltpu.VMEM((experts, cap, feats), bf16),
             pltpu.VMEM((experts * cap, feats), bf16),
             dma((3,)),
+            dma((STRETCH_DEVS,)),
+            dma((STRETCH_DEVS,)),
+            dma((STRETCH_DEVS,)),
+            dma((STRETCH_DEVS,)),
+            dma((1,)),
+            dma((1,)),
             dma((experts,)),
             dma((experts,)),
             dma((experts, span)),
@@ -308,96 +489,18 @@
         compiler_params=pltpu.CompilerParams(
             collective_id=0, has_side_effects=True, vmem_limit_bytes=VMEM_LIMIT
         ),
-        name="experts",
+        name="layer",
     )(
-        expert_in,
-        select,
-        select.T,
-        hidden_state,
+        queries,
+        key_heads,
+        values,
+        residual,
+        ids,
+        norm_gain.reshape(1, feats),
+        router,
         gate_weight,
         up_weight,
         down_weight,
-    )
-
-
-def on_device(
-    queries,
-    key_heads,
-    values,
-    residual,
-    doc_start,
-    norm_gain,
-    router,
-    expert_id,
-    slot_index,
-    gate_weight,
-    up_weight,
-    down_weight,
-):
-    tokens_dev = queries.shape[0]
-    per_group = QH // KVH
-    kv_local = key_heads.shape[1] // HD
-    stretch_len = STRETCH_DEVS * tokens_dev
-    score_scale = 1.0 / math.sqrt(HD)
-    device = lax.axis_index("seq")
-    own_block = (key_heads, values)
-    blocks = []
-    carried = own_block
-    for distance in range(1, STRETCH_DEVS):
-        carried = shifted((carried[0], carried[1]), "seq", 1)
-        blocks.append(carried)
-    ordered = blocks[::-1] + [own_block]
-    key_all = jnp.concatenate([piece[0] for piece in ordered], 0).reshape(-1, kv_local, HD)
-    value_all = jnp.concatenate([piece[1] for piece in ordered], 0).reshape(-1, kv_local, HD)
-    query_view = queries.reshape(tokens_dev, kv_local, per_group, HD)
-    scores = (
-        jnp.einsum("tkgd,skd->kgts", query_view, key_all, preferred_element_type=jnp.float32)
-        * score_scale
-    )
-    query_pos = device * tokens_dev + jnp.arange(tokens_dev, dtype=jnp.int32)
-    key_pos = (device - (STRETCH_DEVS - 1)) * tokens_dev + jnp.arange(
-        STRETCH_DEVS * tokens_dev, dtype=jnp.int32
-    )
-    allowed = (
-        (key_pos[None, :] <= query_pos[:, None])
-        & (key_pos[None, :] // stretch_len == query_pos[:, None] // stretch_len)
-        & (key_pos[None, :] >= doc_start[:, None])
-    )
-    masked = jnp.where(allowed, scores, -jnp.inf)
-    largest = jnp.max(masked, axis=-1, keepdims=True)
-    exponent = jnp.exp(masked - largest)
-    denominator = jnp.sum(exponent, axis=-1, keepdims=True)
-    probabilities = exponent.astype(jnp.bfloat16)
-    attended = jnp.einsum(
-        "kgts,skd->tkgd", probabilities, value_all, preferred_element_type=jnp.float32
-    )
-    attended = (attended / jnp.transpose(denominator, (2, 0, 1, 3))).reshape(tokens_dev, -1)
-    hidden_state = (residual.astype(jnp.float32) + attended).astype(jnp.bfloat16)
-    gained = (hidden_state.astype(jnp.float32) * norm_gain.astype(jnp.float32)).astype(jnp.bfloat16)
-    square_part = jnp.sum(jnp.square(hidden_state.astype(jnp.float32)), axis=1)
-    logit_part = jnp.dot(gained, router, preferred_element_type=jnp.float32)
-    square_sum, logit_sum = lax.psum((square_part, logit_part), "tp")
-    inverse = lax.rsqrt(square_sum / D + 1e-05)
-    experts_all = router.shape[1]
-    chosen = expert_id[:, None] == jnp.arange(experts_all, dtype=jnp.int32)[None, :]
-    picked = jnp.sum(jnp.where(chosen, inverse[:, None] * logit_sum, 0.0), axis=1)
-    factor = inverse * jax.nn.sigmoid(picked)
-    expert_in = (gained.astype(jnp.float32) * factor[:, None]).astype(jnp.bfloat16)
-    capacity = 3 * tokens_dev // (2 * experts_all)
-    slices_per_expert = lax.axis_size("seq") // experts_all
-    place = expert_id * capacity + slot_index
-    select = (
-        jnp.arange(experts_all * capacity, dtype=jnp.int32)[:, None] == place[None, :]
-    ).astype(jnp.bfloat16)
-    return expert_block(
-        expert_in,
-        select,
-        hidden_state,
-        gate_weight,
-        up_weight,
-        down_weight,
-        capacity,
-        slices_per_expert,
     )
 
 

time: 124 us -> 99.8 us (0.80)
  the two profiles are of different devices: /device:TPU:0 before, /device:TPU:8 now
where the time goes in v2:
time: 99.8 us; the launch traced here: 99.5 us
  Pallas kernels  92.3 us (92%)
  local copies, waits for them, and re-layouts  6.6 us (7%)
    pallas_call x1, Pallas kernels, on_device(): pl.pallas_call(functools.partial(layer_kernel, span, cap), out_shape=jax....  92.3 us
    unnamed x2, local copies, waits for them, and re-layouts  3.83 us

profile of v2, /device:TPU:8, one launch (start us, length us, event | category | flops | bytes accessed | tf_op | source)
XLA Modules:
  0.0 99.5 jit_solution(3028428523361180212)
XLA Ops:
  0.0 0.7 add_bitcast_fusion
  0.7 1.5 %stack.20.ids = s32[8,128]{1,0:T(8,128)} concatenate(s32[1,128]{1,0:T(1,128)} %bitcast.10, s32[1,128]{1,0:T(1,128)} %bitcast.4, s32[1,128]{1,0:T(1,128)S(1)} %add_bitcast_fusion, s32[1,128]{1,0:T(1,128)} %bitcast.5, s32[1,128]{1,0:T(1,128)} %bitcast.6, s32[1,128]{1,0:T(1,128)} %bitcast.7, s32[1,128]{1,0:T(1,128)} %bitcast.8, s32[1,128]{1,0:T(1,128)} %bitcast.9), dimensions={0} | concatenate | bytes 8192 | tf_op jit(solution)/shard_map/stack | solution.py:439
  2.2 1.3 %reshape.3.gain = bf16[1,2560]{1,0:T(2,128)(2,1)} reshape(bf16[2560]{0:T(1024)(128)(2,1)} %param.17) | data formatting | bytes 10240 | tf_op jit(solution)/shard_map/reshape | solution.py:499
  3.4 1.9 %copy.13.router = bf16[2560,4]{1,0:T(8,128)(2,1)} copy(bf16[2560,4]{0,1:T(4,128)(2,1)} %param.18) | data formatting | bytes 40960 | tf_op args[6]
  5.3 92.3 %layer.1 = bf16[128,2560]{1,0:T(8,128)(2,1)} custom-call(bf16[128,2560]{1,0:T(8,128)(2,1)} %queries.1, bf16[128,512]{1,0:T(8,128)(2,1)} %keys.1, bf16[128,512]{1,0:T(8,128)(2,1)} %values.1, bf16[128,2560]{1,0:T(8,128)(2,1)} %residual.1, s32[8,128]{1,0:T(8,128)} %stack.20.ids, bf16[1,2560]{1,0:T(2,128)(2,1)} %reshape.3.gain, bf16[2560,4]{1,0:T(8,128)(2,1)} %copy.13.router, ...), custom_call_target="tpu_custom_call" | custom-call | tf_op jit(solution)/shard_map/layer/pallas_call | solution.py:443
  97.6 2.0 %copy.15 = bf16[128,2560]{1,0:T(8,128)(2,1)} copy(bf16[128,2560]{1,0:T(8,128)(2,1)} %layer.1) | data formatting | bytes 1310720

commit v3 on v2

--- a/solution.py
+++ b/solution.py
@@ -36,7 +36,9 @@
     keys,
     values,
     residual,
-    ids,
+    starts,
+    expert_ids,
+    slot_ids,
     gain,
     router,
     gate_hbm,
@@ -91,8 +93,8 @@
     feats = queries.shape[1]
     tokens = queries.shape[0]
     hidden = gate_w.shape[1]
-    ft = 512
-    ht = min(512, hidden)
+    ft = feats // 2
+    ht = min(1024, hidden)
 
     weights = [
         pltpu.make_async_copy(src, dst, w_sem.at[i])
@@ -131,14 +133,15 @@
     below = lax.broadcasted_iota(jnp.int32, (tokens, tokens), 0)
 
     def column(row):
-        spread = jnp.broadcast_to(ids[row : row + 1, :].astype(f32), (tokens, tokens))
+        spread = jnp.broadcast_to(row.astype(f32), (tokens, tokens))
         return jnp.sum(jnp.where(across == below, spread, 0.0), axis=1, keepdims=True).astype(
             jnp.int32
         )
 
-    start_col = column(0)
-    expert_col = column(1)
-    place_col = column(2)
+    place_row = expert_ids[...] * cap + slot_ids[...]
+    start_col = column(starts[...])
+    expert_col = column(expert_ids[...])
+    place_col = column(place_row)
     query_pos = me * tokens + below
     for d in range(STRETCH_DEVS):
         key_pos = (me - d) * tokens + across
@@ -222,7 +225,9 @@
             stat[...] += wide * wide
 
     square = jnp.sum(stat[...], axis=1, keepdims=True)
-    logits = jnp.dot(gained[...], router[...], preferred_element_type=f32)
+    logits = lax.dot_general(
+        gained[...], router[...], (((1,), (1,)), ((), ())), preferred_element_type=f32
+    )
     lane = lax.broadcasted_iota(jnp.int32, (tokens, experts), 1)
     picked = jnp.sum(jnp.where(lane == expert_col, logits, 0.0), axis=1, keepdims=True)
     stat[...] = jnp.where(across == 0, picked, square)
@@ -237,7 +242,7 @@
     stat_copy.start()
     slot_row = lax.broadcasted_iota(jnp.int32, (experts * cap, tokens), 0)
     slot_lane = lax.broadcasted_iota(jnp.int32, (tokens, experts * cap), 1)
-    sel = jnp.where(slot_row == ids[2:3, :], 1.0, 0.0).astype(jnp.bfloat16)
+    sel = jnp.where(slot_row == place_row, 1.0, 0.0).astype(jnp.bfloat16)
     sel_t = jnp.where(slot_lane == place_col, 1.0, 0.0).astype(jnp.bfloat16)
     stat_copy.wait_recv()
     both = stat[...] + stat_recv[...]
@@ -252,23 +257,32 @@
             jnp.bfloat16
         )
 
-    def disp(step):
+    edge = feats // (2 * ft) * ft + (ft if feats % (2 * ft) else 0)
+    halves = ((0, edge), (edge, feats - edge))
+
+    def half(part):
+        return pl.ds(*halves[part])
+
+    def disp(step, part):
         return pltpu.make_async_remote_copy(
-            src_ref=outgoing.at[slots(peer_of(e, step))],
-            dst_ref=rows_in.at[step, slots(j)],
-            send_sem=disp_s.at[step],
-            recv_sem=disp_r.at[step],
+            src_ref=outgoing.at[slots(peer_of(e, step)), half(part)],
+            dst_ref=rows_in.at[step, slots(j), half(part)],
+            send_sem=disp_s.at[step, part],
+            recv_sem=disp_r.at[step, part],
             device_id={"seq": peer_of(e, step) * span + j},
             device_id_type=MESH,
         )
 
-    def fwd(step, d):
-        src = outgoing.at[slots(e)] if step == 0 else rows_in.at[step, slots(j)]
+    def fwd(step, d, part):
+        if step == 0:
+            src = outgoing.at[slots(e), half(part)]
+        else:
+            src = rows_in.at[step, slots(j), half(part)]
         return pltpu.make_async_remote_copy(
             src_ref=src,
-            dst_ref=rows_in.at[step, slots(j)],
-            send_sem=fwd_s.at[step, d],
-            recv_sem=fwd_r.at[step, d],
+            dst_ref=rows_in.at[step, slots(j), half(part)],
+            send_sem=fwd_s.at[step, d, part],
+            recv_sem=fwd_r.at[step, d, part],
             device_id={"seq": e * span + (j + d) % span},
             device_id_type=MESH,
         )
@@ -283,36 +297,43 @@
             device_id_type=MESH,
         )
 
-    def y_copy(step, d):
+    def y_copy(step, d, part):
         return pltpu.make_async_remote_copy(
-            src_ref=piece.at[step, slots((j + d) % span)],
-            dst_ref=piece_recv.at[step, d - 1],
-            send_sem=y_s.at[step, d],
-            recv_sem=y_r.at[step, d],
+            src_ref=piece.at[step, slots((j + d) % span), half(part)],
+            dst_ref=piece_recv.at[step, d - 1, :, half(part)],
+            send_sem=y_s.at[step, d, part],
+            recv_sem=y_r.at[step, d, part],
             device_id={"seq": e * span + (j + d) % span},
             device_id_type=MESH,
         )
 
-    def z_copy(step):
+    def z_copy(step, part):
         return pltpu.make_async_remote_copy(
-            src_ref=back.at[step],
-            dst_ref=returned.at[slots(e)],
-            send_sem=z_s.at[step],
-            recv_sem=z_r.at[step],
+            src_ref=back.at[step, :, half(part)],
+            dst_ref=returned.at[slots(e), half(part)],
+            send_sem=z_s.at[step, part],
+            recv_sem=z_r.at[step, part],
             device_id={"seq": peer_of(e, step) * span + j},
             device_id_type=MESH,
         )
 
+    def dispatch(step):
+        for part in range(2):
+            disp(step, part).start()
+
     def forward(step):
-        if step > 0:
-            disp(step).wait_recv()
-        for d in range(1, span):
-            fwd(step, d).start()
+        for part in range(2):
+            if step > 0:
+                disp(step, part).wait_recv()
+            for d in range(1, span):
+                fwd(step, d, part).start()
+
+    def arrived(step):
+        for part in range(2):
+            for d in range(1, span):
+                fwd(step, d, part).wait_recv()
 
     def gate_up(step):
-        for d in range(1, span):
-            fwd(step, d).wait_recv()
-
         @pl.loop(0, hidden // ht)
         def _(c):
             for weight, base in ((gate_w, 0), (up_w, hidden)):
@@ -337,65 +358,73 @@
             up = own_part[step % 2, :, ups] + part_recv[step, :, ups].astype(jnp.float32)
             act[:, cols] = (jax.nn.silu(gate) * up).astype(jnp.bfloat16)
 
-        @pl.loop(0, feats // ft)
-        def _(c):
-            cols = pl.ds(pl.multiple_of(c * ft, ft), ft)
-            piece[step, :, cols] = jnp.dot(
-                act[...], down_w[:, cols], preferred_element_type=jnp.float32
-            ).astype(jnp.bfloat16)
-
-        for d in range(1, span):
-            y_copy(step, d).start()
+        for part, (low, size) in enumerate(halves):
+
+            @pl.loop(low // ft, (low + size) // ft)
+            def _(c):
+                cols = pl.ds(pl.multiple_of(c * ft, ft), ft)
+                piece[step, :, cols] = jnp.dot(
+                    act[...], down_w[:, cols], preferred_element_type=jnp.float32
+                ).astype(jnp.bfloat16)
+
+            for d in range(1, span):
+                y_copy(step, d, part).start()
 
     def give_back(step):
-        for d in range(1, span):
-            y_copy(step, d).wait_recv()
-
-        @pl.loop(0, feats // ft)
-        def _(c):
-            cols = pl.ds(pl.multiple_of(c * ft, ft), ft)
-            total = piece[step, slots(j), cols].astype(jnp.float32)
+        for part, (low, size) in enumerate(halves):
             for d in range(1, span):
-                total += piece_recv[step, d - 1, :, cols].astype(jnp.float32)
-            if step == 0:
-                returned[slots(e), cols] = total.astype(jnp.bfloat16)
-            else:
-                back[step, :, cols] = total.astype(jnp.bfloat16)
-
-        if step > 0:
-            z_copy(step).start()
-
-    disp(2).start()
-    disp(1).start()
+                y_copy(step, d, part).wait_recv()
+
+            @pl.loop(low // ft, (low + size) // ft)
+            def _(c):
+                cols = pl.ds(pl.multiple_of(c * ft, ft), ft)
+                total = piece[step, slots(j), cols].astype(jnp.float32)
+                for d in range(1, span):
+                    total += piece_recv[step, d - 1, :, cols].astype(jnp.float32)
+                if step == 0:
+                    returned[slots(e), cols] = total.astype(jnp.bfloat16)
+                else:
+                    back[step, :, cols] = total.astype(jnp.bfloat16)
+
+            if step > 0:
+                z_copy(step, part).start()
+
+    dispatch(2)
     forward(0)
     rows_in[0, slots(j)] = outgoing[slots(e)]
     weights[0].wait()
     weights[1].wait()
+    arrived(0)
+    gate_up(0)
+    dispatch(3)
+    dispatch(1)
+    forward(2)
+    weights[2].wait()
+    arrived(2)
+    down(0)
+    gate_up(2)
     forward(1)
-    gate_up(0)
-    disp(3).start()
-    forward(2)
+    forward(3)
+    down(2)
+    arrived(1)
     gate_up(1)
-    weights[2].wait()
-    down(0)
+    give_back(2)
+    arrived(3)
     down(1)
-    forward(3)
-    gate_up(2)
+    gate_up(3)
     give_back(1)
-    down(2)
-    gate_up(3)
-    give_back(2)
     down(3)
     give_back(0)
     give_back(3)
-    for step in range(1, experts):
-        z_copy(step).wait_recv()
-
-    @pl.loop(0, feats // ft)
-    def _(c):
-        cols = pl.ds(pl.multiple_of(c * ft, ft), ft)
-        picked = jnp.dot(sel_t, returned[:, cols], preferred_element_type=jnp.float32)
-        out[:, cols] = (hid[:, cols].astype(jnp.float32) + picked).astype(jnp.bfloat16)
+    for part, (low, size) in enumerate(halves):
+        for step in range(1, experts):
+            z_copy(step, part).wait_recv()
+
+        @pl.loop(low // ft, (low + size) // ft)
+        def _(c):
+            cols = pl.ds(pl.multiple_of(c * ft, ft), ft)
+            picked = jnp.dot(sel_t, returned[:, cols], preferred_element_type=jnp.float32)
+            out[:, cols] = (hid[:, cols].astype(jnp.float32) + picked).astype(jnp.bfloat16)
 
     stat_copy.wait_send()
     for d in range(1, STRETCH_DEVS):
@@ -406,13 +435,14 @@
             kv_copy(values, value_all, v_s, v_r, d).wait_send()
 
     for step in range(experts):
-        if step > 0:
-            disp(step).wait_send()
-            z_copy(step).wait_send()
         tp_copy(step).wait_send()
-        for d in range(1, span):
-            fwd(step, d).wait_send()
-            y_copy(step, d).wait_send()
+        for part in range(2):
+            if step > 0:
+                disp(step, part).wait_send()
+                z_copy(step, part).wait_send()
+            for d in range(1, span):
+                fwd(step, d, part).wait_send()
+                y_copy(step, d, part).wait_send()
 
 
 def on_device(
@@ -436,14 +466,13 @@
     span = lax.axis_size("seq") // experts
     rows = span * cap
     bf16 = jnp.bfloat16
-    ids = jnp.stack([doc_start, expert_id, expert_id * cap + slot_index] + [expert_id] * 5)
     vmem = pl.BlockSpec(memory_space=pltpu.VMEM)
     hbm = pl.BlockSpec(memory_space=pl.ANY)
     dma = pltpu.SemaphoreType.DMA
     return pl.pallas_call(
         functools.partial(layer_kernel, span, cap),
         out_shape=jax.ShapeDtypeStruct((tokens, feats), bf16),
-        in_specs=[vmem] * 7 + [hbm] * 3,
+        in_specs=[vmem] * 9 + [hbm] * 3,
         out_specs=vmem,
         scratch_shapes=[
             pltpu.VMEM((feats, hidden), bf16),
@@ -475,16 +504,16 @@
             dma((STRETCH_DEVS,)),
             dma((1,)),
             dma((1,)),
+            dma((experts, 2)),
+            dma((experts, 2)),
+            dma((experts, span, 2)),
+            dma((experts, span, 2)),
             dma((experts,)),
             dma((experts,)),
-            dma((experts, span)),
-            dma((experts, span)),
-            dma((experts,)),
-            dma((experts,)),
-            dma((experts, span)),
-            dma((experts, span)),
-            dma((experts,)),
-            dma((experts,)),
+            dma((experts, span, 2)),
+            dma((experts, span, 2)),
+            dma((experts, 2)),
+            dma((experts, 2)),
         ],
         compiler_params=pltpu.CompilerParams(
             collective_id=0, has_side_effects=True, vmem_limit_bytes=VMEM_LIMIT
@@ -495,9 +524,11 @@
         key_heads,
         values,
         residual,
-        ids,
+        doc_start.reshape(1, tokens),
+        expert_id.reshape(1, tokens),
+        slot_index.reshape(1, tokens),
         norm_gain.reshape(1, feats),
-        router,
+        router.T,
         gate_weight,
         up_weight,
         down_weight,

time: 99.8 us -> 92.9 us (0.931)
  the two profiles are of different devices: /device:TPU:8 before, /device:TPU:0 now
where the time goes in v3:
time: 92.9 us; the launch traced here: 92.7 us
  Pallas kernels  89.5 us (96%)
  local copies, waits for them, and re-layouts  3.26 us (4%)
    pallas_call x1, Pallas kernels, on_device(): pl.pallas_call(functools.partial(layer_kernel, span, cap), out_shape=jax....  89.5 us
    unnamed x1, local copies, waits for them, and re-layouts  1.97 us

profile of v3, /device:TPU:0, one launch (start us, length us, event | category | flops | bytes accessed | tf_op | source)
XLA Modules:
  0.0 92.7 jit_solution(7316355033513362603)
XLA Ops:
  0.0 1.3 %reshape.15.gain = bf16[1,2560]{1,0:T(2,128)(2,1)} reshape(bf16[2560]{0:T(1024)(128)(2,1)} %param.17) | data formatting | bytes 10240 | tf_op jit(solution)/shard_map/reshape | solution.py:530
  1.3 89.5 %layer.1 = bf16[128,2560]{1,0:T(8,128)(2,1)} custom-call(bf16[128,2560]{1,0:T(8,128)(2,1)} %queries.1, bf16[128,512]{1,0:T(8,128)(2,1)} %keys.1, bf16[128,512]{1,0:T(8,128)(2,1)} %values.1, bf16[128,2560]{1,0:T(8,128)(2,1)} %residual.1, s32[1,128]{1,0:T(1,128)} %bitcast.5, s32[1,128]{1,0:T(1,128)} %bitcast.6, s32[1,128]{1,0:T(1,128)} %bitcast.7, ...), custom_call_target="tpu_custom_call" | custom-call | tf_op jit(solution)/shard_map/layer/pallas_call | solution.py:472
  90.8 2.0 %copy.14 = bf16[128,2560]{1,0:T(8,128)(2,1)} copy(bf16[128,2560]{1,0:T(8,128)(2,1)} %layer.1) | data formatting | bytes 1310720

commit v4 on v3

--- a/solution.py
+++ b/solution.py
@@ -162,10 +162,7 @@
             device_id_type=MESH,
         )
 
-    for src, dst, send, recv in (
-        (keys, key_all, k_s, k_r),
-        (values, value_all, v_s, v_r),
-    ):
+    def send_on(src, dst, send, recv):
         for d in range(STRETCH_DEVS - 1, 0, -1):
 
             @pl.when(place + d < STRETCH_DEVS)
@@ -175,6 +172,15 @@
             @pl.when(place < d)
             def _():
                 dst[d] = jnp.zeros_like(src)
+
+    send_on(keys, key_all, k_s, k_r)
+    for d in range(1, STRETCH_DEVS):
+
+        @pl.when(place + d < STRETCH_DEVS)
+        def _():
+            kv_copy(keys, key_all, k_s, k_r, d).wait_send()
+
+    send_on(values, value_all, v_s, v_r)
 
     for d in range(1, STRETCH_DEVS):
 
@@ -431,7 +437,6 @@
 
         @pl.when(place + d < STRETCH_DEVS)
         def _():
-            kv_copy(keys, key_all, k_s, k_r, d).wait_send()
             kv_copy(values, value_all, v_s, v_r, d).wait_send()
 
     for step in range(experts):

time: 92.9 us -> 94.7 us (1.019)
  Pallas kernels: 89.5 us -> 91.2 us
    pallas_call x1, Pallas kernels: 89.5 us -> 91.2 us  [on_device(): pl.pallas_call(functools.partial(layer_kernel, span, cap), out_shape=jax....]
where the time goes in v4:
time: 94.7 us; the launch traced here: 94.5 us
  Pallas kernels  91.2 us (96%)
  local copies, waits for them, and re-layouts  3.26 us (3%)
    pallas_call x1, Pallas kernels, on_device(): pl.pallas_call(functools.partial(layer_kernel, span, cap), out_shape=jax....  91.2 us
    unnamed x1, local copies, waits for them, and re-layouts  1.97 us

profile of v4, /device:TPU:0, one launch (start us, length us, event | category | flops | bytes accessed | tf_op | source)
XLA Modules:
  0.0 94.5 jit_solution(13625972784896680004)
XLA Ops:
  0.0 1.3 %reshape.15.gain = bf16[1,2560]{1,0:T(2,128)(2,1)} reshape(bf16[2560]{0:T(1024)(128)(2,1)} %param.17) | data formatting | bytes 10240 | tf_op jit(solution)/shard_map/reshape | solution.py:535
  1.3 91.2 %layer.1 = bf16[128,2560]{1,0:T(8,128)(2,1)} custom-call(bf16[128,2560]{1,0:T(8,128)(2,1)} %queries.1, bf16[128,512]{1,0:T(8,128)(2,1)} %keys.1, bf16[128,512]{1,0:T(8,128)(2,1)} %values.1, bf16[128,2560]{1,0:T(8,128)(2,1)} %residual.1, s32[1,128]{1,0:T(1,128)} %bitcast.5, s32[1,128]{1,0:T(1,128)} %bitcast.6, s32[1,128]{1,0:T(1,128)} %bitcast.7, ...), custom_call_target="tpu_custom_call" | custom-call | tf_op jit(solution)/shard_map/layer/pallas_call | solution.py:477
  92.5 2.0 %copy.14 = bf16[128,2560]{1,0:T(8,128)(2,1)} copy(bf16[128,2560]{1,0:T(8,128)(2,1)} %layer.1) | data formatting | bytes 1310720
